TPU v7x, 32 devices: a whole 2x2x4 slice. The times are simulated.
32 devices in a mesh: row: 2 (over x), col: 4 (over y, core), layer: 4 (over z).
Axes of the slice: x: 2, y: 2, z: 4, core: 2. Of those that a mesh axis runs over, the one named last changes fastest.
Arguments:
- amplitudes: bfloat16 [2, 4, 128, 8192], P('row', 'col', None, 'layer'), may hold values from -6 to 6
- tile_mask: int32 [2, 4, 128, 32], P('row', 'col', None, 'layer'), may hold values 0 or 1
- owners: int32 [2, 4, 128, 1], P('row', 'col'), may hold values from 0 to 7; in each aligned block of 128 rows (0 to 127, 128 to 255, ..., all dimensions but the last counted through in order) at most 32 rows name the same one
- col_panels: bfloat16 [2, 4, 4, 256, 512], P('row', 'col', 'layer'), may hold values from -0.0625 to 0.0625
- row_panels: bfloat16 [2, 4, 4, 256, 512], P('row', 'col', 'layer'), may hold values from -0.0625 to 0.0625
Outputs:
- residual: bfloat16 [2, 4, 128, 512], P('row', 'col', None, 'layer')
Inputs may be any that keep to these rules, and one draw needn't show every extreme that they name: `owners`: among the 128 rows of one grid position at most 32 name the same destination, and in every draw some grid position names one destination exactly 32 times.
All inputs are finite; a program needn't handle non-finite values. No bound on the sum of `tile_mask` on one device may be relied on, other than what follows from the above.
Results may differ from a plain program's by a relative error of at most 0.013.
Values may be sent and summed in bfloat16 or wider, within the bound.
A program may use at most 64 MiB of HBM per device.

v0:
```python
import jax
import jax.numpy as jnp
from jax import lax
from jax.sharding import PartitionSpec as P


def from_behind(x, axis, by):
    length = lax.axis_size(axis)
    return lax.ppermute(x, axis, [(i, (i + by) % length) for i in range(length)])


def body(amplitudes, tile_mask, owners, col_panels, row_panels):
    rows_here = amplitudes.shape[2]
    width_k = amplitudes.shape[3]
    blocks = tile_mask.shape[3]
    tile_width = width_k // blocks
    half_blocks = blocks // 2
    grid_rows = lax.axis_size("row")
    grid_cols = lax.axis_size("col")
    peer_count = grid_rows * grid_cols
    capacity = max(2, 2 * rows_here // peer_count)
    slot_count = peer_count * capacity
    keep_mask = tile_mask[0, 0].astype(jnp.bfloat16)
    masked = (
        amplitudes[0, 0].reshape(rows_here, blocks, tile_width) * keep_mask[:, :, None]
    ).reshape(rows_here, width_k)
    destined = owners[0, 0, :, 0]
    onehot = (destined[:, None] == jnp.arange(peer_count, dtype=jnp.int32)[None, :]).astype(
        jnp.int32
    )
    slot_rank = jnp.sum((jnp.cumsum(onehot, axis=0) - onehot) * onehot, axis=1)
    slot_index = destined * capacity + slot_rank
    source_of = (
        jnp.zeros((slot_count,), jnp.int32)
        .at[slot_index]
        .set(jnp.arange(rows_here, dtype=jnp.int32))
    )
    filled = jnp.zeros((slot_count,), jnp.int32).at[slot_index].set(1)
    outgoing = jnp.take(masked, source_of, axis=0) * filled[:, None].astype(jnp.bfloat16)
    arrived = lax.all_to_all(
        outgoing.reshape(peer_count, capacity, width_k),
        ("row", "col"),
        split_axis=0,
        concat_axis=0,
        tiled=True,
    )
    arrived = arrived.reshape(slot_count, width_k)
    col_panel = col_panels[0, 0, 0]
    row_panel = row_panels[0, 0, 0]
    partial_value = jnp.zeros((slot_count, col_panel.shape[1]), jnp.float32)
    for position in range(half_blocks):
        if position > 0:
            col_panel = from_behind(col_panel, "col", -1)
            row_panel = from_behind(row_panel, "row", -1)
        col_block = arrived[:, position * tile_width : (position + 1) * tile_width]
        row_block = arrived[
            :, (half_blocks + position) * tile_width : (half_blocks + position + 1) * tile_width
        ]
        partial_value = partial_value + jnp.dot(
            col_block, col_panel, preferred_element_type=jnp.float32
        )
        partial_value = partial_value + jnp.dot(
            row_block, row_panel, preferred_element_type=jnp.float32
        )
    rounded = partial_value.astype(jnp.bfloat16)
    returned = lax.all_to_all(
        rounded.reshape(peer_count, capacity, rounded.shape[1]),
        ("row", "col"),
        split_axis=0,
        concat_axis=0,
        tiled=True,
    )
    own_rows = jnp.take(returned.reshape(slot_count, rounded.shape[1]), slot_index, axis=0)
    result = lax.psum_scatter(
        own_rows.astype(jnp.float32).astype(jnp.bfloat16), "layer", scatter_dimension=1, tiled=True
    )
    return result.reshape(1, 1, rows_here, result.shape[1])


def solution(mesh):
    return jax.shard_map(
        body,
        mesh=mesh,
        in_specs=(
            P("row", "col", None, "layer"),
            P("row", "col", None, "layer"),
            P("row", "col", None, None),
            P("row", "col", "layer", None, None),
            P("row", "col", "layer", None, None),
        ),
        out_specs=P("row", "col", None, "layer"),
        check_vma=False,
    )
```

profile of v0, /device:TPU:0, one launch (start us, length us, event | category | flops | bytes accessed | tf_op | source)
XLA Modules:
  0.0 94.4 jit_solution(12136936639021499265)
XLA Ops:
  6.5 0.7 copy-done.4
  7.3 0.2 reduce_window_sum.11
  7.5 0.2 select_reduce_fusion
  7.7 1.0 %scatter_custom_fusion = s32[256]{0:T(256)S(1)} fusion(s32[128]{0:T(128)S(1)} %fusion.17, s32[128]{0:T(128)S(1)} %iota.7, s32[]{:T(128)} %constant.23.clone.1), kind=kCustom, calls=%fused_computation.42 | custom fusion | bytes 1028 | tf_op jit(solution)/shard_map/scatter | solution.py:36
  8.7 0.6 copy-done.3
  9.5 0.2 mul.53
  9.9 1.0 %scatter_custom_fusion.1 = s32[256]{0:T(256)S(1)} fusion(s32[128]{0:T(128)S(1)} %fusion.17, s32[128]{0:T(128)S(1)} %broadcast.53, s32[]{:T(128)} %constant.23.clone.1), kind=kCustom, calls=%fused_computation.40 | custom fusion | bytes 1028 | tf_op jit(solution)/shard_map/scatter | solution.py:38
  11.0 1.4 %gather_fusion = bf16[256,2048]{1,0:T(8,128)(2,1)S(1)} fusion(bf16[128,2048]{1,0:T(8,128)(2,1)S(1)} %bitcast_multiply_fusion, s32[1024]{0:T(1024)S(1)} %pad_clamp_fusion.1), kind=kCustom, calls=%fused_computation | custom fusion | bytes 2098176 | tf_op jit(solution)/shard_map/jit(_take)/gather | solution.py:39
  12.4 1.1 %select_multiply_fusion = bf16[8,32,2048]{2,1,0:T(8,128)(2,1)} fusion(bf16[8,32,2048]{2,1,0:T(8,128)(2,1)S(1)} %bitcast.36, pred[8,32]{1,0:T(8,128)(4,1)S(1)} %broadcast_in_dim.33, bf16[8,32]{1,0:T(8,128)(2,1)S(1)} %mul.56), kind=kLoop, calls=%fused_computation.12 | loop fusion | flops 1048576 | bytes 2097920 | tf_op jit(solution)/shard_map/mul | solution.py:39
  13.5 5.3 %all-to-all-start = ((bf16[8,32,2048]{2,1,0:T(8,128)(2,1)}), bf16[8,32,2048]{2,1,0:T(8,128)(2,1)S(1)}, u32[]{:S(2)}, u32[]{:S(2)}) async-start(bf16[8,32,2048]{2,1,0:T(8,128)(2,1)} %select_multiply_fusion), calls=%async_computation | async-start | bytes 2097152 | tf_op jit(solution)/shard_map/all_to_all | solution.py:40
  18.9 2.0 %collective-permute-start.1 = (bf16[256,512]{1,0:T(8,128)(2,1)S(1)}, bf16[256,512]{1,0:T(8,128)(2,1)S(1)}, u32[]{:S(2)}, u32[]{:S(2)}) collective-permute-start(bf16[256,512]{1,0:T(8,128)(2,1)S(1)} %bitcast.49), channel_id=1, source_target_pairs={{0,16},{16,0},{1,17},{17,1},{2,18},{18,2},{3,19},{19,3},{4,20},{20... | collective-permute-start | bytes 786440 | tf_op jit(solution)/shard_map/ppermute | solution.py:9
  20.9 0.9 collective-permute-start
  21.8 17.1 %collective-permute-done.1 = bf16[256,512]{1,0:T(8,128)(2,1)S(1)} collective-permute-done((bf16[256,512]{1,0:T(8,128)(2,1)S(1)}, bf16[256,512]{1,0:T(8,128)(2,1)S(1)}, u32[]{:S(2)}, u32[]{:S(2)}) %collective-permute-start.1) | collective-permute-done | bytes 262176 | tf_op jit(solution)/shard_map/ppermute | solution.py:9
  38.9 0.4 collective-permute-start.3
  39.3 0.6 collective-permute-start.2
  39.9 6.9 %collective-permute-done.3 = bf16[256,512]{1,0:T(8,128)(2,1)S(1)} collective-permute-done((bf16[256,512]{1,0:T(8,128)(2,1)S(1)}, bf16[256,512]{1,0:T(8,128)(2,1)S(1)}, u32[]{:S(2)}, u32[]{:S(2)}) %collective-permute-start.3) | collective-permute-done | bytes 262176 | tf_op jit(solution)/shard_map/ppermute | solution.py:9
  46.8 0.7 collective-permute-start.5
  47.5 0.2 fusion.14
  47.7 0.2 fusion.10
  47.9 0.2 fusion.7
  48.2 0.2 convolution_add_fusion.3
  48.4 5.3 %collective-permute-done.5 = bf16[256,512]{1,0:T(8,128)(2,1)S(1)} collective-permute-done((bf16[256,512]{1,0:T(8,128)(2,1)S(1)}, bf16[256,512]{1,0:T(8,128)(2,1)S(1)}, u32[]{:S(2)}, u32[]{:S(2)}) %collective-permute-start.5) | collective-permute-done | bytes 262176 | tf_op jit(solution)/shard_map/ppermute | solution.py:9
  53.7 0.2 fusion.4
  54.0 0.2 fusion.2
  54.2 0.2 fusion.1
  54.4 0.9 fusion.3
  55.4 3.4 %all-to-all-start.1 = ((bf16[8,32,512]{2,1,0:T(8,128)(2,1)}), bf16[8,32,512]{2,1,0:T(8,128)(2,1)S(1)}, u32[]{:S(2)}, u32[]{:S(2)}) async-start(bf16[8,32,512]{2,1,0:T(8,128)(2,1)} %bitcast.10), calls=%async_computation.1 | async-start | bytes 524288 | tf_op jit(solution)/shard_map/all_to_all | solution.py:66
  58.9 5.9 %all-to-all-done.1 = bf16[8,32,512]{2,1,0:T(8,128)(2,1)S(1)} async-done(((bf16[8,32,512]{2,1,0:T(8,128)(2,1)}), bf16[8,32,512]{2,1,0:T(8,128)(2,1)S(1)}, u32[]{:S(2)}, u32[]{:S(2)}) %all-to-all-start.1) | async-done | bytes 262176 | tf_op jit(solution)/shard_map/all_to_all | solution.py:66
  64.8 0.8 gather_fusion.1
  65.7 0.7 copy.8
  66.5 19.6 %reduce-scatter.4.cloned.1.call-done = bf16[128,128]{1,0:T(8,128)(2,1)} async-done(((bf16[512,128]{1,0:T(8,128)(2,1)}), bf16[128,128]{1,0:T(8,128)(2,1)}) %reduce-scatter.4.cloned.1.call-update) | async-done | bytes 32784
  86.1 1.5 %copy.9 = bf16[128,128]{1,0:T(8,128)(2,1)} copy(bf16[128,128]{0,1:T(8,128)(2,1)} %bitcast.50) | data formatting | bytes 65536
  (32 shorter events, 0.8 us)
Async XLA Ops:
  6.5 0.7 copy-start.4
  8.6 0.7 copy-start.3
  9.7 1.3 %copy-start = (bf16[1,1,128,2048]{3,2,1,0:T(8,128)(2,1)S(1)}, bf16[1,1,128,2048]{3,2,1,0:T(8,128)(2,1)}, u32[]{:S(2)}) copy-start(bf16[1,1,128,2048]{3,2,1,0:T(8,128)(2,1)} %param.5) | copy-start | bytes 1572868
  13.5 5.3 %copy-start.2 = (bf16[1,1,1,256,512]{4,3,2,1,0:T(8,128)(2,1)S(1)}, bf16[1,1,1,256,512]{4,3,2,1,0:T(8,128)(2,1)}, u32[]{:S(2)}) copy-start(bf16[1,1,1,256,512]{4,3,2,1,0:T(8,128)(2,1)} %param.9) | copy-start | bytes 786436
  13.5 7.3 %copy-start.1 = (bf16[1,1,1,256,512]{4,3,2,1,0:T(8,128)(2,1)S(1)}, bf16[1,1,1,256,512]{4,3,2,1,0:T(8,128)(2,1)}, u32[]{:S(2)}) copy-start(bf16[1,1,1,256,512]{4,3,2,1,0:T(8,128)(2,1)} %param.8) | copy-start | bytes 786436
  13.5 33.9 %all-to-all-start = ((bf16[8,32,2048]{2,1,0:T(8,128)(2,1)}), bf16[8,32,2048]{2,1,0:T(8,128)(2,1)S(1)}, u32[]{:S(2)}, u32[]{:S(2)}) async-start(bf16[8,32,2048]{2,1,0:T(8,128)(2,1)} %select_multiply_fusion), calls=%async_computation | async-start | bytes 2097152 | tf_op jit(solution)/shard_map/all_to_all | solution.py:40
  18.9 20.1 %collective-permute-start.1 = (bf16[256,512]{1,0:T(8,128)(2,1)S(1)}, bf16[256,512]{1,0:T(8,128)(2,1)S(1)}, u32[]{:S(2)}, u32[]{:S(2)}) collective-permute-start(bf16[256,512]{1,0:T(8,128)(2,1)S(1)} %bitcast.49), channel_id=1, source_target_pairs={{0,16},{16,0},{1,17},{17,1},{2,18},{18,2},{3,19},{19,3},{4,20},{20... | collective-permute-start | bytes 786440 | tf_op jit(solution)/shard_map/ppermute | solution.py:9
  20.9 18.5 %collective-permute-start = (bf16[256,512]{1,0:T(8,128)(2,1)S(1)}, bf16[256,512]{1,0:T(8,128)(2,1)S(1)}, u32[]{:S(2)}, u32[]{:S(2)}) collective-permute-start(bf16[256,512]{1,0:T(8,128)(2,1)S(1)} %bitcast.48), channel_id=1, source_target_pairs={{0,12},{4,0},{8,4},{12,8},{1,13},{5,1},{9,5},{13,9},{2,14},{6,2},{... | collective-permute-start | bytes 786440 | tf_op jit(solution)/shard_map/ppermute | solution.py:9
  38.9 7.8 %collective-permute-start.3 = (bf16[256,512]{1,0:T(8,128)(2,1)S(1)}, bf16[256,512]{1,0:T(8,128)(2,1)S(1)}, u32[]{:S(2)}, u32[]{:S(2)}) collective-permute-start(bf16[256,512]{1,0:T(8,128)(2,1)S(1)} %collective-permute-done.1), channel_id=1, source_target_pairs={{0,16},{16,0},{1,17},{17,1},{2,18},{18,2},{3,19},{19,3},{4,20},{20... | collective-permute-start | bytes 786440 | tf_op jit(solution)/shard_map/ppermute | solution.py:9
  39.3 8.1 %collective-permute-start.2 = (bf16[256,512]{1,0:T(8,128)(2,1)S(1)}, bf16[256,512]{1,0:T(8,128)(2,1)S(1)}, u32[]{:S(2)}, u32[]{:S(2)}) collective-permute-start(bf16[256,512]{1,0:T(8,128)(2,1)S(1)} %collective-permute-done), channel_id=1, source_target_pairs={{0,12},{4,0},{8,4},{12,8},{1,13},{5,1},{9,5},{13,9},{2,14},{6,2},{... | collective-permute-start | bytes 786440 | tf_op jit(solution)/shard_map/ppermute | solution.py:9
  46.8 6.9 %collective-permute-start.5 = (bf16[256,512]{1,0:T(8,128)(2,1)S(1)}, bf16[256,512]{1,0:T(8,128)(2,1)S(1)}, u32[]{:S(2)}, u32[]{:S(2)}) collective-permute-start(bf16[256,512]{1,0:T(8,128)(2,1)S(1)} %collective-permute-done.3), channel_id=1, source_target_pairs={{0,16},{16,0},{1,17},{17,1},{2,18},{18,2},{3,19},{19,3},{4,20},{20... | collective-permute-start | bytes 786440 | tf_op jit(solution)/shard_map/ppermute | solution.py:9
  47.5 7.0 %collective-permute-start.4 = (bf16[256,512]{1,0:T(8,128)(2,1)S(1)}, bf16[256,512]{1,0:T(8,128)(2,1)S(1)}, u32[]{:S(2)}, u32[]{:S(2)}) collective-permute-start(bf16[256,512]{1,0:T(8,128)(2,1)S(1)} %collective-permute-done.2), channel_id=1, source_target_pairs={{0,12},{4,0},{8,4},{12,8},{1,13},{5,1},{9,5},{13,9},{2,14},{6,2},{... | collective-permute-start | bytes 786440 | tf_op jit(solution)/shard_map/ppermute | solution.py:9
  55.4 9.4 %all-to-all-start.1 = ((bf16[8,32,512]{2,1,0:T(8,128)(2,1)}), bf16[8,32,512]{2,1,0:T(8,128)(2,1)S(1)}, u32[]{:S(2)}, u32[]{:S(2)}) async-start(bf16[8,32,512]{2,1,0:T(8,128)(2,1)} %bitcast.10), calls=%async_computation.1 | async-start | bytes 524288 | tf_op jit(solution)/shard_map/all_to_all | solution.py:66
  58.8 27.3 %reduce-scatter.4.cloned.1.call-start = ((), (), s32[]{:S(2)}) async-start(), calls=%async_computation.3 | async-start | bytes 163840
Sparse Core Ops, SparseCore 0:
  66.6 19.4 reduce-scatter.3
where the time goes:
time: 94.8 us; the launch traced here: 94.4 us
  waiting for transfers between devices  54.8 us (58%)
  between operations  13.6 us (14%)
  starting transfers between devices  13.4 us (14%)
  local copies, waits for them, and re-layouts  8.3 us (9%)
  matrix products  2.52 us (3%)
  other arithmetic  1.76 us (2%)
    ppermute x6, waiting for transfers between devices, from_behind(): lax.ppermute(x, axis, [(i, (i + by) % length) for i in range(length)])  29.3 us
    unnamed x2, waiting for transfers between devices  19.6 us
    all_to_all x1, waiting for transfers between devices, body(): lax.all_to_all(rounded.reshape(peer_count, capacity, rounded.shape[1]), (...  5.9 us
    all_to_all x1, starting transfers between devices, body(): lax.all_to_all(outgoing.reshape(peer_count, capacity, width_k), ('row', '...  5.3 us
    ppermute x6, starting transfers between devices, from_behind(): lax.ppermute(x, axis, [(i, (i + by) % length) for i in range(length)])  4.64 us
    unnamed x13, local copies, waits for them, and re-layouts  3.64 us
    all_to_all x1, starting transfers between devices, body(): lax.all_to_all(rounded.reshape(peer_count, capacity, rounded.shape[1]), (...  3.41 us
  transfers between devices with their start and end apart: 9, of which 5 were waited for; matrix products, arithmetic and copies ran while one was open for 2% of the time, Pallas kernels for 0%

commit v1 on v0

--- a/solution.py
+++ b/solution.py
@@ -1,7 +1,14 @@
+import functools
+
 import jax
 import jax.numpy as jnp
 from jax import lax
+from jax.experimental import pallas as pl
+from jax.experimental.pallas import tpu as pltpu
 from jax.sharding import PartitionSpec as P
+
+MESH = pl.DeviceIdType.MESH
+GROUPS = 2
 
 
 def from_behind(x, axis, by):
@@ -9,7 +16,7 @@
     return lax.ppermute(x, axis, [(i, (i + by) % length) for i in range(length)])
 
 
-def body(amplitudes, tile_mask, owners, col_panels, row_panels):
+def routed(amplitudes, tile_mask, owners, col_panels, row_panels):
     rows_here = amplitudes.shape[2]
     width_k = amplitudes.shape[3]
     blocks = tile_mask.shape[3]
@@ -25,16 +32,11 @@
         amplitudes[0, 0].reshape(rows_here, blocks, tile_width) * keep_mask[:, :, None]
     ).reshape(rows_here, width_k)
     destined = owners[0, 0, :, 0]
-    onehot = (destined[:, None] == jnp.arange(peer_count, dtype=jnp.int32)[None, :]).astype(
-        jnp.int32
-    )
-    slot_rank = jnp.sum((jnp.cumsum(onehot, axis=0) - onehot) * onehot, axis=1)
+    ids = jnp.arange(rows_here, dtype=jnp.int32)
+    earlier = (destined[:, None] == destined[None, :]) & (ids[None, :] < ids[:, None])
+    slot_rank = jnp.sum(earlier.astype(jnp.int32), axis=1)
     slot_index = destined * capacity + slot_rank
-    source_of = (
-        jnp.zeros((slot_count,), jnp.int32)
-        .at[slot_index]
-        .set(jnp.arange(rows_here, dtype=jnp.int32))
-    )
+    source_of = jnp.zeros((slot_count,), jnp.int32).at[slot_index].set(ids)
     filled = jnp.zeros((slot_count,), jnp.int32).at[slot_index].set(1)
     outgoing = jnp.take(masked, source_of, axis=0) * filled[:, None].astype(jnp.bfloat16)
     arrived = lax.all_to_all(
@@ -77,9 +79,213 @@
     return result.reshape(1, 1, rows_here, result.shape[1])
 
 
+def kernel(layers, amp, mask, own, colp, rowp, out, panels, lhs, xs, xr, outb, inbox,
+           ysend, yrecv, ssend, srecv, fsend, frecv, xsend, xrecv, osend, irecv):
+    rows, tw, nw = amp.shape[0], colp.shape[0], colp.shape[1]
+    gw, cw = nw // GROUPS, nw // layers
+    x, q, z = lax.axis_index("row"), lax.axis_index("col"), lax.axis_index("layer")
+    core = lax.rem(q, 2)
+    sib, yq = q + 1 - 2 * core, lax.rem(q + 2, 4)
+    ysib = yq + 1 - 2 * core
+    cols = [q, sib, yq, ysib]
+    other = 1 - x
+
+    barrier = pltpu.get_barrier_semaphore()
+
+    def greet(device):
+        pl.semaphore_signal(barrier, inc=1, device_id=device, device_id_type=MESH)
+
+    greet((x, yq, z))
+    greet((x, sib, z))
+    for n in range(layers):
+        greet((other, q, n))
+
+        @pl.when(n != z)
+        def _():
+            greet((x, q, n))
+
+    def copy(src, dst, s, r, device):
+        return pltpu.make_async_remote_copy(
+            src_ref=src, dst_ref=dst, send_sem=s, recv_sem=r, device_id=device, device_id_type=MESH
+        )
+
+    def group(g):
+        return pl.ds(g * gw, gw)
+
+    own_panels = [colp, rowp]
+    to_y = [[copy(own_panels[k].at[:, group(g)], panels.at[k, 1, :, group(g)], ysend.at[k, g],
+                  yrecv.at[k, g], (x, yq, z)) for k in range(2)] for g in range(GROUPS)]
+    to_sib = [copy(own_panels[k], panels.at[k, 0], ssend.at[k], srecv.at[k], (x, sib, z))
+              for k in range(2)]
+    onward = [[copy(panels.at[k, 1, :, group(g)], panels.at[k, 2, :, group(g)], fsend.at[k, g],
+                    frecv.at[k, g], (x, sib, z)) for k in range(2)] for g in range(GROUPS)]
+    code_row = pl.ds(0, 128 + 2 * tw)
+    to_x = [
+        copy(xs.at[:, code_row], xr, xsend.at[0], xrecv.at[0], (other, q, z)),
+        copy(xs.at[:, pl.ds(128 + 2 * tw, 4 * tw)], lhs.at[pl.ds(rows, rows), pl.ds(0, 4 * tw)],
+             xsend.at[1], xrecv.at[1], (other, q, z)),
+    ]
+
+    def wide(a):
+        return jnp.concatenate([a] * (tw // 128), axis=1)
+
+    def flag(cond):
+        return wide(cond.astype(jnp.float32).astype(jnp.bfloat16))
+
+    dest = jnp.broadcast_to(own[...], (rows, 128))
+    dest_row = jnp.where(dest >= 4, 1, 0)
+    dest_col = dest - 4 * dest_row
+    here, there = flag(dest_row == x), flag(dest_row != x)
+
+    def block(m):
+        keep = jnp.broadcast_to(mask[:, m : m + 1], (rows, 128))
+        return amp[:, m * tw : (m + 1) * tw] * flag(keep != 0)
+
+    xs[:, :128] = dest_col.astype(jnp.float32).astype(jnp.bfloat16)
+    own_row = []
+    for m in range(2):
+        even, odd = block(4 + 2 * m), block(5 + 2 * m)
+        own_row.append(even * here + odd * there)
+        xs[:, 128 + m * tw : 128 + (m + 1) * tw] = odd * here + even * there
+    col_blocks = [block(s) for s in range(4)]
+    for j in range(4):
+        met = sum(col_blocks[s] * flag(dest_col == lax.rem(cols[j] + 4 - s, 4)) for s in range(4))
+        lhs[:rows, j * tw : (j + 1) * tw] = met * here
+        xs[:, 128 + (2 + j) * tw : 128 + (3 + j) * tw] = met * there
+
+    pl.semaphore_wait(barrier, 2 * layers + 1)
+    for c in to_sib:
+        c.start()
+    for c in to_y[0]:
+        c.start()
+    for c in to_x:
+        c.start()
+    for g in range(1, GROUPS):
+        for c in to_y[g]:
+            c.start()
+
+    for j in range(4):
+        meets = flag(dest_col == cols[j])
+        for m in range(2):
+            lhs[:rows, (4 + 2 * j + m) * tw : (5 + 2 * j + m) * tw] = own_row[m] * meets
+
+    for c in to_sib:
+        c.wait_recv()
+    for c in to_x:
+        c.wait_recv()
+    code = xr[:, :128].astype(jnp.float32)
+    for j in range(4):
+        meets = flag(code == cols[j].astype(jnp.float32))
+        for m in range(2):
+            lhs[rows:, (4 + 2 * j + m) * tw : (5 + 2 * j + m) * tw] = (
+                xr[:, 128 + m * tw : 128 + (m + 1) * tw] * meets
+            )
+
+    def result(n, side):
+        return copy(outb.at[side, n], inbox.at[z, side], osend.at[side, n], irecv.at[z, side],
+                    (x if side == 0 else other, q, n))
+
+    for g in range(GROUPS):
+        for k in range(2):
+            to_y[g][k].wait_recv()
+            onward[g][k].start()
+        total = jnp.zeros((2 * rows, gw), jnp.float32)
+        for j in range(4):
+            if j == 3:
+                for k in range(2):
+                    onward[g][k].wait_recv()
+            col = colp[:, g * gw : (g + 1) * gw] if j == 0 else panels[0, j - 1, :, g * gw : (g + 1) * gw]
+            row = rowp[:, g * gw : (g + 1) * gw] if j == 0 else panels[1, j - 1, :, g * gw : (g + 1) * gw]
+            total += jnp.dot(lhs[:, j * tw : (j + 1) * tw], col, preferred_element_type=jnp.float32)
+            for m in range(2):
+                at = (4 + 2 * j + m) * tw
+                total += jnp.dot(lhs[:, at : at + tw], row, preferred_element_type=jnp.float32)
+        total = total.astype(jnp.bfloat16)
+        for i in range(layers // GROUPS):
+            n = g * (layers // GROUPS) + i
+            outb[0, n] = total[:rows, i * cw : (i + 1) * cw]
+            outb[1, n] = total[rows:, i * cw : (i + 1) * cw]
+            result(n, 1).start()
+
+            @pl.when(n != z)
+            def _():
+                result(n, 0).start()
+
+            @pl.when(n == z)
+            def _():
+                inbox[n, 0] = outb[0, n]
+
+    def arrived(n, side):
+        copy(outb.at[side, n], inbox.at[n, side], osend.at[side, n], irecv.at[n, side],
+             (x if side == 0 else other, q, n)).wait_recv()
+
+    for n in range(layers):
+        arrived(n, 1)
+
+        @pl.when(n != z)
+        def _():
+            arrived(n, 0)
+
+    result_sum = jnp.zeros((rows, cw), jnp.float32)
+    for n in range(layers):
+        result_sum += inbox[n, 0].astype(jnp.float32) + inbox[n, 1].astype(jnp.float32)
+    out[...] = result_sum.astype(out.dtype)
+
+    for c in to_sib + to_x:
+        c.wait_send()
+    for g in range(GROUPS):
+        for c in to_y[g] + onward[g]:
+            c.wait_send()
+    for n in range(layers):
+        result(n, 1).wait_send()
+
+        @pl.when(n != z)
+        def _():
+            result(n, 0).wait_send()
+
+
+def crossed(amplitudes, tile_mask, owners, col_panels, row_panels):
+    layers = lax.axis_size("layer")
+    rows, width_k = amplitudes.shape[2:]
+    tw, nw = col_panels.shape[3:]
+    blocks = tile_mask.shape[3]
+    cw = nw // layers
+    dma = pltpu.SemaphoreType.DMA
+    bf16 = jnp.bfloat16
+    vmem = pl.BlockSpec(memory_space=pltpu.VMEM)
+    result = pl.pallas_call(
+        functools.partial(kernel, layers),
+        out_shape=jax.ShapeDtypeStruct((rows, cw), bf16),
+        in_specs=[vmem] * 5,
+        out_specs=vmem,
+        scratch_shapes=[
+            pltpu.VMEM((2, 3, tw, nw), bf16),
+            pltpu.VMEM((2 * rows, 12 * tw), bf16),
+            pltpu.VMEM((rows, 128 + 6 * tw), bf16),
+            pltpu.VMEM((rows, 128 + 2 * tw), bf16),
+            pltpu.VMEM((2, layers, rows, cw), bf16),
+            pltpu.VMEM((layers, 2, rows, cw), bf16),
+            dma((2, GROUPS)), dma((2, GROUPS)), dma((2,)), dma((2,)),
+            dma((2, GROUPS)), dma((2, GROUPS)), dma((2,)), dma((2,)),
+            dma((2, layers)), dma((layers, 2)),
+        ],
+        compiler_params=pltpu.CompilerParams(
+            collective_id=0, has_side_effects=True, vmem_limit_bytes=32 * 1024 * 1024
+        ),
+    )(
+        amplitudes.reshape(rows, width_k),
+        tile_mask.reshape(rows, blocks),
+        owners.reshape(rows, 1),
+        col_panels.reshape(tw, nw),
+        row_panels.reshape(tw, nw),
+    )
+    return result.reshape(1, 1, rows, cw)
+
+
 def solution(mesh):
+    small = mesh.shape["row"] == 2 and mesh.shape["col"] == 4
     return jax.shard_map(
-        body,
+        crossed if small else routed,
         mesh=mesh,
         in_specs=(
             P("row", "col", None, "layer"),

time: 94.8 us -> 31.3 us (0.33)
  the two profiles are of different devices: /device:TPU:0 before, /device:TPU:25 now
where the time goes in v1:
time: 31.3 us; the launch traced here: 31 us
  Pallas kernels  25.9 us (83%)
  local copies, waits for them, and re-layouts  5.1 us (16%)
    pallas_call x1, Pallas kernels, crossed(): pl.pallas_call(functools.partial(kernel, layers), out_shape=jax.ShapeDtyp...  25.9 us
    unnamed x12, local copies, waits for them, and re-layouts  4.99 us

profile of v1, /device:TPU:25, one launch (start us, length us, event | category | flops | bytes accessed | tf_op | source)
XLA Modules:
  0.0 31.0 jit_solution(15652860659580323821)
XLA Ops:
  0.0 0.0 copy-start.3
  0.0 0.7 %copy-done.3 = s32[1,1,128,8]{2,3,1,0:T(8,128)S(1)} copy-done((s32[1,1,128,8]{2,3,1,0:T(8,128)S(1)}, s32[1,1,128,8]{2,3,1,0:T(8,128)}, u32[]{:S(2)}) %copy-start.3) | copy-done | bytes 4120
  0.7 0.1 copy.6
  0.8 0.0 copy-start.4
  0.8 0.7 %copy-done.4 = s32[1,1,128,1]{2,3,1,0:T(1,128)S(1)} copy-done((s32[1,1,128,1]{2,3,1,0:T(1,128)S(1)}, s32[1,1,128,1]{2,3,1,0:T(1,128)}, u32[]{:S(2)}) %copy-start.4) | copy-done | bytes 536
  1.4 0.1 copy.7.own
  1.6 0.0 copy-start
  1.6 1.0 %copy-done = bf16[1,1,128,2048]{3,2,1,0:T(8,128)(2,1)S(1)} copy-done((bf16[1,1,128,2048]{3,2,1,0:T(8,128)(2,1)S(1)}, bf16[1,1,128,2048]{3,2,1,0:T(8,128)(2,1)}, u32[]{:S(2)}) %copy-start) | copy-done | bytes 524312
  2.6 0.0 copy-start.1
  2.6 0.9 %copy-done.1 = bf16[1,1,1,256,512]{4,3,2,1,0:T(8,128)(2,1)S(1)} copy-done((bf16[1,1,1,256,512]{4,3,2,1,0:T(8,128)(2,1)S(1)}, bf16[1,1,1,256,512]{4,3,2,1,0:T(8,128)(2,1)}, u32[]{:S(2)}) %copy-start.1) | copy-done | bytes 262168
  3.5 0.0 copy-start.2
  3.6 0.9 %copy-done.2 = bf16[1,1,1,256,512]{4,3,2,1,0:T(8,128)(2,1)S(1)} copy-done((bf16[1,1,1,256,512]{4,3,2,1,0:T(8,128)(2,1)S(1)}, bf16[1,1,1,256,512]{4,3,2,1,0:T(8,128)(2,1)}, u32[]{:S(2)}) %copy-start.2) | copy-done | bytes 262168
  4.5 25.9 %shard_map.55 = bf16[128,128]{1,0:T(8,128)(2,1)S(1)} custom-call(bf16[128,2048]{1,0:T(8,128)(2,1)S(1)} %bitcast.6, s32[128,8]{1,0:T(8,128)S(1)} %bitcast.9, s32[128,1]{1,0:T(8,128)S(1)} %copy.7.own, bf16[256,512]{1,0:T(8,128)(2,1)S(1)} %bitcast.7, bf16[256,512]{1,0:T(8,128)(2,1)S(1)} %bitcast.8), custom_call_target="tpu_custom_call" | custom-call | tf_op jit(solution)/shard_map/pallas_call | solution.py:256
  30.4 0.6 %copy.9 = bf16[1,1,128,128]{3,2,1,0:T(8,128)(2,1)} copy(bf16[1,1,128,128]{3,2,1,0:T(8,128)(2,1)S(1)} %bitcast.10) | data formatting | bytes 65536
Async XLA Ops:
  0.0 0.7 %copy-start.3 = (s32[1,1,128,8]{2,3,1,0:T(8,128)S(1)}, s32[1,1,128,8]{2,3,1,0:T(8,128)}, u32[]{:S(2)}) copy-start(s32[1,1,128,8]{2,3,1,0:T(8,128)} %param.6) | copy-start | bytes 12292
  0.8 0.7 %copy-start.4 = (s32[1,1,128,1]{2,3,1,0:T(1,128)S(1)}, s32[1,1,128,1]{2,3,1,0:T(1,128)}, u32[]{:S(2)}) copy-start(s32[1,1,128,1]{2,3,1,0:T(1,128)} %param.7) | copy-start | bytes 1540
  1.6 1.0 %copy-start = (bf16[1,1,128,2048]{3,2,1,0:T(8,128)(2,1)S(1)}, bf16[1,1,128,2048]{3,2,1,0:T(8,128)(2,1)}, u32[]{:S(2)}) copy-start(bf16[1,1,128,2048]{3,2,1,0:T(8,128)(2,1)} %param.5) | copy-start | bytes 1572868
  2.6 0.9 %copy-start.1 = (bf16[1,1,1,256,512]{4,3,2,1,0:T(8,128)(2,1)S(1)}, bf16[1,1,1,256,512]{4,3,2,1,0:T(8,128)(2,1)}, u32[]{:S(2)}) copy-start(bf16[1,1,1,256,512]{4,3,2,1,0:T(8,128)(2,1)} %param.8) | copy-start | bytes 786436
  3.5 0.9 %copy-start.2 = (bf16[1,1,1,256,512]{4,3,2,1,0:T(8,128)(2,1)S(1)}, bf16[1,1,1,256,512]{4,3,2,1,0:T(8,128)(2,1)}, u32[]{:S(2)}) copy-start(bf16[1,1,1,256,512]{4,3,2,1,0:T(8,128)(2,1)} %param.9) | copy-start | bytes 786436

commit v2 on v1

--- a/solution.py
+++ b/solution.py
@@ -8,7 +8,7 @@
 from jax.sharding import PartitionSpec as P
 
 MESH = pl.DeviceIdType.MESH
-GROUPS = 2
+GROUPS = 4
 
 
 def from_behind(x, axis, by):
@@ -79,8 +79,8 @@
     return result.reshape(1, 1, rows_here, result.shape[1])
 
 
-def kernel(layers, amp, mask, own, colp, rowp, out, panels, lhs, xs, xr, outb, inbox,
-           ysend, yrecv, ssend, srecv, fsend, frecv, xsend, xrecv, osend, irecv):
+def kernel(layers, amp_hbm, mask_hbm, own_hbm, col_hbm, row_hbm, out, amp, mask, own, colp, rowp,
+           panels, lhs, xs, xr, codes, codes_in, outb, inbox, load, ysend, yrecv, ssend, srecv, fsend, frecv, xsend, xrecv, osend, irecv):
     rows, tw, nw = amp.shape[0], colp.shape[0], colp.shape[1]
     gw, cw = nw // GROUPS, nw // layers
     x, q, z = lax.axis_index("row"), lax.axis_index("col"), lax.axis_index("layer")
@@ -112,17 +112,22 @@
     def group(g):
         return pl.ds(g * gw, gw)
 
-    own_panels = [colp, rowp]
+    loads = [pltpu.make_async_copy(a, b, load.at[i]) for i, (a, b) in enumerate(
+        [(own_hbm, own), (mask_hbm, mask), (amp_hbm, amp), (col_hbm, colp), (row_hbm, rowp)])]
+    for c in loads:
+        c.start()
+
+    own_panels = [col_hbm, row_hbm]
     to_y = [[copy(own_panels[k].at[:, group(g)], panels.at[k, 1, :, group(g)], ysend.at[k, g],
                   yrecv.at[k, g], (x, yq, z)) for k in range(2)] for g in range(GROUPS)]
     to_sib = [copy(own_panels[k], panels.at[k, 0], ssend.at[k], srecv.at[k], (x, sib, z))
               for k in range(2)]
     onward = [[copy(panels.at[k, 1, :, group(g)], panels.at[k, 2, :, group(g)], fsend.at[k, g],
                     frecv.at[k, g], (x, sib, z)) for k in range(2)] for g in range(GROUPS)]
-    code_row = pl.ds(0, 128 + 2 * tw)
     to_x = [
-        copy(xs.at[:, code_row], xr, xsend.at[0], xrecv.at[0], (other, q, z)),
-        copy(xs.at[:, pl.ds(128 + 2 * tw, 4 * tw)], lhs.at[pl.ds(rows, rows), pl.ds(0, 4 * tw)],
+        copy(codes, codes_in, xsend.at[2], xrecv.at[2], (other, q, z)),
+        copy(xs.at[:, pl.ds(0, tw)], xr, xsend.at[0], xrecv.at[0], (other, q, z)),
+        copy(xs.at[:, pl.ds(tw, 4 * tw)], lhs.at[pl.ds(rows, rows), pl.ds(0, 4 * tw)],
              xsend.at[1], xrecv.at[1], (other, q, z)),
     ]
 
@@ -132,54 +137,58 @@
     def flag(cond):
         return wide(cond.astype(jnp.float32).astype(jnp.bfloat16))
 
-    dest = jnp.broadcast_to(own[...], (rows, 128))
+    def down(row):
+        return jnp.transpose(jnp.broadcast_to(row.astype(jnp.float32), (128, rows)))
+
+    pl.semaphore_wait(barrier, 2 * layers + 1)
+    for c in to_y[0] + to_sib:
+        c.start()
+    for g in range(1, GROUPS):
+        for c in to_y[g]:
+            c.start()
+
+    for c in loads[:3]:
+        c.wait()
+    dest = down(own[...]).astype(jnp.int32)
     dest_row = jnp.where(dest >= 4, 1, 0)
     dest_col = dest - 4 * dest_row
     here, there = flag(dest_row == x), flag(dest_row != x)
 
     def block(m):
-        keep = jnp.broadcast_to(mask[:, m : m + 1], (rows, 128))
-        return amp[:, m * tw : (m + 1) * tw] * flag(keep != 0)
-
-    xs[:, :128] = dest_col.astype(jnp.float32).astype(jnp.bfloat16)
-    own_row = []
-    for m in range(2):
-        even, odd = block(4 + 2 * m), block(5 + 2 * m)
-        own_row.append(even * here + odd * there)
-        xs[:, 128 + m * tw : 128 + (m + 1) * tw] = odd * here + even * there
+        return amp[:, m * tw : (m + 1) * tw] * wide(down(mask[m : m + 1]).astype(jnp.bfloat16))
+
+    codes[...] = jnp.broadcast_to(own[...] - 4 * jnp.where(own[...] >= 4, 1, 0), codes.shape).astype(
+        jnp.float32
+    ).astype(jnp.bfloat16)
+    f32 = jnp.float32
+    even = (block(4).astype(f32) + block(6).astype(f32)).astype(jnp.bfloat16)
+    odd = (block(5).astype(f32) + block(7).astype(f32)).astype(jnp.bfloat16)
+    own_row = even * here + odd * there
+    xs[:, :tw] = odd * here + even * there
+    to_x[0].start()
+    to_x[1].start()
     col_blocks = [block(s) for s in range(4)]
     for j in range(4):
         met = sum(col_blocks[s] * flag(dest_col == lax.rem(cols[j] + 4 - s, 4)) for s in range(4))
         lhs[:rows, j * tw : (j + 1) * tw] = met * here
-        xs[:, 128 + (2 + j) * tw : 128 + (3 + j) * tw] = met * there
-
-    pl.semaphore_wait(barrier, 2 * layers + 1)
-    for c in to_sib:
-        c.start()
-    for c in to_y[0]:
-        c.start()
-    for c in to_x:
-        c.start()
-    for g in range(1, GROUPS):
-        for c in to_y[g]:
-            c.start()
+        xs[:, (1 + j) * tw : (2 + j) * tw] = met * there
+
+    to_x[2].start()
 
     for j in range(4):
         meets = flag(dest_col == cols[j])
-        for m in range(2):
-            lhs[:rows, (4 + 2 * j + m) * tw : (5 + 2 * j + m) * tw] = own_row[m] * meets
-
+        lhs[:rows, (4 + j) * tw : (5 + j) * tw] = own_row * meets
+
+    for c in loads[3:]:
+        c.wait()
     for c in to_sib:
         c.wait_recv()
     for c in to_x:
         c.wait_recv()
-    code = xr[:, :128].astype(jnp.float32)
+    code = down(codes_in[...][:1])
     for j in range(4):
         meets = flag(code == cols[j].astype(jnp.float32))
-        for m in range(2):
-            lhs[rows:, (4 + 2 * j + m) * tw : (5 + 2 * j + m) * tw] = (
-                xr[:, 128 + m * tw : 128 + (m + 1) * tw] * meets
-            )
+        lhs[rows:, (4 + j) * tw : (5 + j) * tw] = xr[...] * meets
 
     def result(n, side):
         return copy(outb.at[side, n], inbox.at[z, side], osend.at[side, n], irecv.at[z, side],
@@ -197,9 +206,9 @@
             col = colp[:, g * gw : (g + 1) * gw] if j == 0 else panels[0, j - 1, :, g * gw : (g + 1) * gw]
             row = rowp[:, g * gw : (g + 1) * gw] if j == 0 else panels[1, j - 1, :, g * gw : (g + 1) * gw]
             total += jnp.dot(lhs[:, j * tw : (j + 1) * tw], col, preferred_element_type=jnp.float32)
-            for m in range(2):
-                at = (4 + 2 * j + m) * tw
-                total += jnp.dot(lhs[:, at : at + tw], row, preferred_element_type=jnp.float32)
+            total += jnp.dot(
+                lhs[:, (4 + j) * tw : (5 + j) * tw], row, preferred_element_type=jnp.float32
+            )
         total = total.astype(jnp.bfloat16)
         for i in range(layers // GROUPS):
             n = g * (layers // GROUPS) + i
@@ -256,26 +265,33 @@
     result = pl.pallas_call(
         functools.partial(kernel, layers),
         out_shape=jax.ShapeDtypeStruct((rows, cw), bf16),
-        in_specs=[vmem] * 5,
+        in_specs=[pl.BlockSpec(memory_space=pltpu.HBM)] * 5,
         out_specs=vmem,
         scratch_shapes=[
+            pltpu.VMEM((rows, width_k), bf16),
+            pltpu.VMEM((blocks, rows), jnp.int32),
+            pltpu.VMEM((1, rows), jnp.int32),
+            pltpu.VMEM((tw, nw), bf16),
+            pltpu.VMEM((tw, nw), bf16),
             pltpu.VMEM((2, 3, tw, nw), bf16),
-            pltpu.VMEM((2 * rows, 12 * tw), bf16),
-            pltpu.VMEM((rows, 128 + 6 * tw), bf16),
-            pltpu.VMEM((rows, 128 + 2 * tw), bf16),
+            pltpu.VMEM((2 * rows, 8 * tw), bf16),
+            pltpu.VMEM((rows, 5 * tw), bf16),
+            pltpu.VMEM((rows, tw), bf16),
+            pltpu.VMEM((16, rows), bf16),
+            pltpu.VMEM((16, rows), bf16),
             pltpu.VMEM((2, layers, rows, cw), bf16),
             pltpu.VMEM((layers, 2, rows, cw), bf16),
-            dma((2, GROUPS)), dma((2, GROUPS)), dma((2,)), dma((2,)),
-            dma((2, GROUPS)), dma((2, GROUPS)), dma((2,)), dma((2,)),
+            dma((5,)), dma((2, GROUPS)), dma((2, GROUPS)), dma((2,)), dma((2,)),
+            dma((2, GROUPS)), dma((2, GROUPS)), dma((3,)), dma((3,)),
             dma((2, layers)), dma((layers, 2)),
         ],
         compiler_params=pltpu.CompilerParams(
-            collective_id=0, has_side_effects=True, vmem_limit_bytes=32 * 1024 * 1024
+            collective_id=0, has_side_effects=True, vmem_limit_bytes=60 * 1024 * 1024
         ),
     )(
         amplitudes.reshape(rows, width_k),
-        tile_mask.reshape(rows, blocks),
-        owners.reshape(rows, 1),
+        tile_mask.reshape(rows, blocks).T,
+        owners.reshape(1, rows),
         col_panels.reshape(tw, nw),
         row_panels.reshape(tw, nw),
     )

time: 31.3 us -> 26.2 us (0.84)
  local copies, waits for them, and re-layouts: 5.1 us -> 1.38 us
  Pallas kernels: 25.9 us -> 24.6 us
    unnamed x12 -> x1, local copies, waits for them, and re-layouts: 4.99 us -> 1.38 us
    pallas_call x1, Pallas kernels: 25.9 us -> 24.6 us  [crossed(): pl.pallas_call(functools.partial(kernel, layers), out_shape=jax.ShapeDtyp...]
where the time goes in v2:
time: 26.2 us; the launch traced here: 26 us
  Pallas kernels  24.6 us (94%)
  local copies, waits for them, and re-layouts  1.38 us (5%)
    pallas_call x1, Pallas kernels, crossed(): pl.pallas_call(functools.partial(kernel, layers), out_shape=jax.ShapeDtyp...  24.6 us
    unnamed x1, local copies, waits for them, and re-layouts  1.38 us

profile of v2, /device:TPU:25, one launch (start us, length us, event | category | flops | bytes accessed | tf_op | source)
XLA Modules:
  0.0 26.0 jit_solution(6192622719560777839)
XLA Ops:
  0.0 24.6 %shard_map.55 = bf16[128,128]{1,0:T(8,128)(2,1)} custom-call(bf16[128,2048]{1,0:T(8,128)(2,1)} %bitcast.8, s32[8,128]{1,0:T(8,128)} %bitcast.12, s32[1,128]{1,0:T(1,128)} %bitcast.13, bf16[256,512]{1,0:T(8,128)(2,1)} %bitcast.9, bf16[256,512]{1,0:T(8,128)(2,1)} %bitcast.10), custom_call_target="tpu_custom_call" | custom-call | tf_op jit(solution)/shard_map/pallas_call | solution.py:265
  24.6 1.4 %copy.7 = bf16[1,1,128,128]{3,2,1,0:T(8,128)(2,1)} copy(bf16[1,1,128,128]{3,2,1,0:T(8,128)(2,1)} %bitcast.11) | data formatting | bytes 65536

commit v3 on v2

--- a/solution.py
+++ b/solution.py
@@ -8,7 +8,6 @@
 from jax.sharding import PartitionSpec as P
 
 MESH = pl.DeviceIdType.MESH
-GROUPS = 4
 
 
 def from_behind(x, axis, by):
@@ -80,9 +79,9 @@
 
 
 def kernel(layers, amp_hbm, mask_hbm, own_hbm, col_hbm, row_hbm, out, amp, mask, own, colp, rowp,
-           panels, lhs, xs, xr, codes, codes_in, outb, inbox, load, ysend, yrecv, ssend, srecv, fsend, frecv, xsend, xrecv, osend, irecv):
+           panels, lhs, xs, xr, codes, codes_in, outb, inbox, answer, ready, load, ysend, yrecv, ssend, srecv, fsend, frecv, xsend, xrecv, osend, irecv):
     rows, tw, nw = amp.shape[0], colp.shape[0], colp.shape[1]
-    gw, cw = nw // GROUPS, nw // layers
+    cw = nw // layers
     x, q, z = lax.axis_index("row"), lax.axis_index("col"), lax.axis_index("layer")
     core = lax.rem(q, 2)
     sib, yq = q + 1 - 2 * core, lax.rem(q + 2, 4)
@@ -90,40 +89,49 @@
     cols = [q, sib, yq, ysib]
     other = 1 - x
 
+    loads = [pltpu.make_async_copy(a, b, load.at[i]) for i, (a, b) in enumerate(
+        [(own_hbm, own), (mask_hbm, mask), (amp_hbm, amp), (col_hbm, colp), (row_hbm, rowp)])]
+    for c in loads:
+        c.start()
+
     barrier = pltpu.get_barrier_semaphore()
 
     def greet(device):
         pl.semaphore_signal(barrier, inc=1, device_id=device, device_id_type=MESH)
 
-    greet((x, yq, z))
-    greet((x, sib, z))
-    for n in range(layers):
-        greet((other, q, n))
-
-        @pl.when(n != z)
-        def _():
-            greet((x, q, n))
+    odd = lax.rem(x + q // 2 + core, 2) == 1
+    near = [(x, yq, z), (x, sib, z), (other, q, z)]
+
+    @pl.when(odd)
+    def _():
+        for device in near:
+            greet(device)
+
+    @pl.when(jnp.logical_not(odd))
+    def _():
+        pl.semaphore_wait(barrier, len(near))
+        for device in near:
+            pl.semaphore_signal(answer, inc=1, device_id=device, device_id_type=MESH)
 
     def copy(src, dst, s, r, device):
         return pltpu.make_async_remote_copy(
             src_ref=src, dst_ref=dst, send_sem=s, recv_sem=r, device_id=device, device_id_type=MESH
         )
 
+    hops = [k for k in range(1, layers)]
+    hops = sorted(hops, key=lambda k: (k != layers // 2, k)) + [0]
+    keepers = [lax.rem(z + k, layers) for k in hops]
+
     def group(g):
-        return pl.ds(g * gw, gw)
-
-    loads = [pltpu.make_async_copy(a, b, load.at[i]) for i, (a, b) in enumerate(
-        [(own_hbm, own), (mask_hbm, mask), (amp_hbm, amp), (col_hbm, colp), (row_hbm, rowp)])]
-    for c in loads:
-        c.start()
+        return pl.ds(pl.multiple_of(keepers[g] * cw, cw), cw)
 
     own_panels = [col_hbm, row_hbm]
     to_y = [[copy(own_panels[k].at[:, group(g)], panels.at[k, 1, :, group(g)], ysend.at[k, g],
-                  yrecv.at[k, g], (x, yq, z)) for k in range(2)] for g in range(GROUPS)]
+                  yrecv.at[k, g], (x, yq, z)) for k in range(2)] for g in range(layers)]
     to_sib = [copy(own_panels[k], panels.at[k, 0], ssend.at[k], srecv.at[k], (x, sib, z))
               for k in range(2)]
     onward = [[copy(panels.at[k, 1, :, group(g)], panels.at[k, 2, :, group(g)], fsend.at[k, g],
-                    frecv.at[k, g], (x, sib, z)) for k in range(2)] for g in range(GROUPS)]
+                    frecv.at[k, g], (x, sib, z)) for k in range(2)] for g in range(layers)]
     to_x = [
         copy(codes, codes_in, xsend.at[2], xrecv.at[2], (other, q, z)),
         copy(xs.at[:, pl.ds(0, tw)], xr, xsend.at[0], xrecv.at[0], (other, q, z)),
@@ -140,12 +148,23 @@
     def down(row):
         return jnp.transpose(jnp.broadcast_to(row.astype(jnp.float32), (128, rows)))
 
-    pl.semaphore_wait(barrier, 2 * layers + 1)
+    @pl.when(odd)
+    def _():
+        pl.semaphore_wait(answer, len(near))
+
     for c in to_y[0] + to_sib:
         c.start()
-    for g in range(1, GROUPS):
+    for g in range(1, layers):
         for c in to_y[g]:
             c.start()
+
+    @pl.when(odd)
+    def _():
+        for n in range(layers):
+
+            @pl.when(n != z)
+            def _():
+                greet((x, q, n))
 
     for c in loads[:3]:
         c.wait()
@@ -161,10 +180,10 @@
         jnp.float32
     ).astype(jnp.bfloat16)
     f32 = jnp.float32
-    even = (block(4).astype(f32) + block(6).astype(f32)).astype(jnp.bfloat16)
-    odd = (block(5).astype(f32) + block(7).astype(f32)).astype(jnp.bfloat16)
-    own_row = even * here + odd * there
-    xs[:, :tw] = odd * here + even * there
+    evens = (block(4).astype(f32) + block(6).astype(f32)).astype(jnp.bfloat16)
+    odds = (block(5).astype(f32) + block(7).astype(f32)).astype(jnp.bfloat16)
+    own_row = evens * here + odds * there
+    xs[:, :tw] = odds * here + evens * there
     to_x[0].start()
     to_x[1].start()
     col_blocks = [block(s) for s in range(4)]
@@ -190,67 +209,58 @@
         meets = flag(code == cols[j].astype(jnp.float32))
         lhs[rows:, (4 + j) * tw : (5 + j) * tw] = xr[...] * meets
 
-    def result(n, side):
-        return copy(outb.at[side, n], inbox.at[z, side], osend.at[side, n], irecv.at[z, side],
-                    (x if side == 0 else other, q, n))
-
-    for g in range(GROUPS):
+    @pl.when(odd)
+    def _():
+        pl.semaphore_wait(barrier, layers - 1)
+        pl.semaphore_signal(ready, inc=1, device_id=(other, q, z), device_id_type=MESH)
+
+    @pl.when(jnp.logical_not(odd))
+    def _():
+        pl.semaphore_wait(ready, 1)
+
+    def result(g, side):
+        return copy(outb.at[side, g], inbox.at[side, g], osend.at[side, g], irecv.at[side, g],
+                    (x if side == 0 else other, q, keepers[g]))
+
+    for g in range(layers):
         for k in range(2):
             to_y[g][k].wait_recv()
             onward[g][k].start()
-        total = jnp.zeros((2 * rows, gw), jnp.float32)
+        total = jnp.zeros((2 * rows, cw), jnp.float32)
         for j in range(4):
             if j == 3:
                 for k in range(2):
                     onward[g][k].wait_recv()
-            col = colp[:, g * gw : (g + 1) * gw] if j == 0 else panels[0, j - 1, :, g * gw : (g + 1) * gw]
-            row = rowp[:, g * gw : (g + 1) * gw] if j == 0 else panels[1, j - 1, :, g * gw : (g + 1) * gw]
+            col = colp[:, group(g)] if j == 0 else panels[0, j - 1, :, group(g)]
+            row = rowp[:, group(g)] if j == 0 else panels[1, j - 1, :, group(g)]
             total += jnp.dot(lhs[:, j * tw : (j + 1) * tw], col, preferred_element_type=jnp.float32)
             total += jnp.dot(
                 lhs[:, (4 + j) * tw : (5 + j) * tw], row, preferred_element_type=jnp.float32
             )
-        total = total.astype(jnp.bfloat16)
-        for i in range(layers // GROUPS):
-            n = g * (layers // GROUPS) + i
-            outb[0, n] = total[:rows, i * cw : (i + 1) * cw]
-            outb[1, n] = total[rows:, i * cw : (i + 1) * cw]
-            result(n, 1).start()
-
-            @pl.when(n != z)
-            def _():
-                result(n, 0).start()
-
-            @pl.when(n == z)
-            def _():
-                inbox[n, 0] = outb[0, n]
-
-    def arrived(n, side):
-        copy(outb.at[side, n], inbox.at[n, side], osend.at[side, n], irecv.at[n, side],
-             (x if side == 0 else other, q, n)).wait_recv()
-
-    for n in range(layers):
-        arrived(n, 1)
-
-        @pl.when(n != z)
-        def _():
-            arrived(n, 0)
-
-    result_sum = jnp.zeros((rows, cw), jnp.float32)
-    for n in range(layers):
-        result_sum += inbox[n, 0].astype(jnp.float32) + inbox[n, 1].astype(jnp.float32)
-    out[...] = result_sum.astype(out.dtype)
+        outb[1, g] = total[rows:].astype(jnp.bfloat16)
+        result(g, 1).start()
+        outb[0, g] = total[:rows].astype(jnp.bfloat16)
+        if g < layers - 1:
+            result(g, 0).start()
+
+    kept = outb[0, layers - 1].astype(jnp.float32)
+    for g in range(layers):
+        if g < layers - 1:
+            result(g, 0).wait_recv()
+            kept += inbox[0, g].astype(jnp.float32)
+        result(g, 1).wait_recv()
+        kept += inbox[1, g].astype(jnp.float32)
+    out[...] = kept.astype(out.dtype)
 
     for c in to_sib + to_x:
         c.wait_send()
-    for g in range(GROUPS):
+    for g in range(layers):
         for c in to_y[g] + onward[g]:
             c.wait_send()
-    for n in range(layers):
-        result(n, 1).wait_send()
-
-        @pl.when(n != z)
-        def _():
-            result(n, 0).wait_send()
+    for g in range(layers):
+        result(g, 1).wait_send()
+        if g < layers - 1:
+            result(g, 0).wait_send()
 
 
 def crossed(amplitudes, tile_mask, owners, col_panels, row_panels):
@@ -280,10 +290,11 @@
             pltpu.VMEM((16, rows), bf16),
             pltpu.VMEM((16, rows), bf16),
             pltpu.VMEM((2, layers, rows, cw), bf16),
-            pltpu.VMEM((layers, 2, rows, cw), bf16),
-            dma((5,)), dma((2, GROUPS)), dma((2, GROUPS)), dma((2,)), dma((2,)),
-            dma((2, GROUPS)), dma((2, GROUPS)), dma((3,)), dma((3,)),
-            dma((2, layers)), dma((layers, 2)),
+            pltpu.VMEM((2, layers, rows, cw), bf16),
+            pltpu.SemaphoreType.REGULAR, pltpu.SemaphoreType.REGULAR,
+            dma((5,)), dma((2, layers)), dma((2, layers)), dma((2,)), dma((2,)),
+            dma((2, layers)), dma((2, layers)), dma((3,)), dma((3,)),
+            dma((2, layers)), dma((2, layers)),
         ],
         compiler_params=pltpu.CompilerParams(
             collective_id=0, has_side_effects=True, vmem_limit_bytes=60 * 1024 * 1024

time: 26.2 us -> 25.8 us (0.985)
  the two profiles are of different devices: /device:TPU:25 before, /device:TPU:0 now
where the time goes in v3:
time: 25.8 us; the launch traced here: 25.6 us
  Pallas kernels  24.2 us (94%)
  local copies, waits for them, and re-layouts  1.38 us (5%)
    pallas_call x1, Pallas kernels, crossed(): pl.pallas_call(functools.partial(kernel, layers), out_shape=jax.ShapeDtyp...  24.2 us
    unnamed x1, local copies, waits for them, and re-layouts  1.38 us

profile of v3, /device:TPU:0, one launch (start us, length us, event | category | flops | bytes accessed | tf_op | source)
XLA Modules:
  0.0 25.6 jit_solution(13792225000961408520)
XLA Ops:
  0.0 24.2 %shard_map.55 = bf16[128,128]{1,0:T(8,128)(2,1)} custom-call(bf16[128,2048]{1,0:T(8,128)(2,1)} %bitcast.8, s32[8,128]{1,0:T(8,128)} %bitcast.12, s32[1,128]{1,0:T(1,128)} %bitcast.13, bf16[256,512]{1,0:T(8,128)(2,1)} %bitcast.9, bf16[256,512]{1,0:T(8,128)(2,1)} %bitcast.10), custom_call_target="tpu_custom_call" | custom-call | tf_op jit(solution)/shard_map/pallas_call | solution.py:275
  24.2 1.4 %copy.7 = bf16[1,1,128,128]{3,2,1,0:T(8,128)(2,1)} copy(bf16[1,1,128,128]{3,2,1,0:T(8,128)(2,1)} %bitcast.11) | data formatting | bytes 65536

commit v4 on v3

--- a/solution.py
+++ b/solution.py
@@ -198,8 +198,14 @@
         meets = flag(dest_col == cols[j])
         lhs[:rows, (4 + j) * tw : (5 + j) * tw] = own_row * meets
 
+    def pass_on(g):
+        for k in range(2):
+            to_y[g][k].wait_recv()
+            onward[g][k].start()
+
     for c in loads[3:]:
         c.wait()
+    pass_on(0)
     for c in to_sib:
         c.wait_recv()
     for c in to_x:
@@ -223,9 +229,8 @@
                     (x if side == 0 else other, q, keepers[g]))
 
     for g in range(layers):
-        for k in range(2):
-            to_y[g][k].wait_recv()
-            onward[g][k].start()
+        if g + 1 < layers:
+            pass_on(g + 1)
         total = jnp.zeros((2 * rows, cw), jnp.float32)
         for j in range(4):
             if j == 3:

time: 25.8 us -> 25.3 us (0.981)
  Pallas kernels: 24.2 us -> 23.8 us
    pallas_call x1, Pallas kernels: 24.2 us -> 23.8 us  [crossed(): pl.pallas_call(functools.partial(kernel, layers), out_shape=jax.ShapeDtyp...]
where the time goes in v4:
time: 25.3 us; the launch traced here: 25.1 us
  Pallas kernels  23.8 us (94%)
  local copies, waits for them, and re-layouts  1.38 us (5%)
    pallas_call x1, Pallas kernels, crossed(): pl.pallas_call(functools.partial(kernel, layers), out_shape=jax.ShapeDtyp...  23.8 us
    unnamed x1, local copies, waits for them, and re-layouts  1.38 us

profile of v4, /device:TPU:0, one launch (start us, length us, event | category | flops | bytes accessed | tf_op | source)
XLA Modules:
  0.0 25.1 jit_solution(17203236670330813349)
XLA Ops:
  0.0 23.8 %shard_map.55 = bf16[128,128]{1,0:T(8,128)(2,1)} custom-call(bf16[128,2048]{1,0:T(8,128)(2,1)} %bitcast.8, s32[8,128]{1,0:T(8,128)} %bitcast.12, s32[1,128]{1,0:T(1,128)} %bitcast.13, bf16[256,512]{1,0:T(8,128)(2,1)} %bitcast.9, bf16[256,512]{1,0:T(8,128)(2,1)} %bitcast.10), custom_call_target="tpu_custom_call" | custom-call | tf_op jit(solution)/shard_map/pallas_call | solution.py:280
  23.8 1.4 %copy.7 = bf16[1,1,128,128]{3,2,1,0:T(8,128)(2,1)} copy(bf16[1,1,128,128]{3,2,1,0:T(8,128)(2,1)} %bitcast.11) | data formatting | bytes 65536

commit v5 on v4

--- a/solution.py
+++ b/solution.py
@@ -215,15 +215,6 @@
         meets = flag(code == cols[j].astype(jnp.float32))
         lhs[rows:, (4 + j) * tw : (5 + j) * tw] = xr[...] * meets
 
-    @pl.when(odd)
-    def _():
-        pl.semaphore_wait(barrier, layers - 1)
-        pl.semaphore_signal(ready, inc=1, device_id=(other, q, z), device_id_type=MESH)
-
-    @pl.when(jnp.logical_not(odd))
-    def _():
-        pl.semaphore_wait(ready, 1)
-
     def result(g, side):
         return copy(outb.at[side, g], inbox.at[side, g], osend.at[side, g], irecv.at[side, g],
                     (x if side == 0 else other, q, keepers[g]))
@@ -243,6 +234,17 @@
                 lhs[:, (4 + j) * tw : (5 + j) * tw], row, preferred_element_type=jnp.float32
             )
         outb[1, g] = total[rows:].astype(jnp.bfloat16)
+        if g == 0:
+
+            @pl.when(odd)
+            def _():
+                pl.semaphore_wait(barrier, layers - 1)
+                pl.semaphore_signal(ready, inc=1, device_id=(other, q, z), device_id_type=MESH)
+
+            @pl.when(jnp.logical_not(odd))
+            def _():
+                pl.semaphore_wait(ready, 1)
+
         result(g, 1).start()
         outb[0, g] = total[:rows].astype(jnp.bfloat16)
         if g < layers - 1:

time: 25.3 us -> 25.3 us (level)
  no operation moved by 1% of the time
where the time goes in v5:
time: 25.3 us; the launch traced here: 25.1 us
  Pallas kernels  23.8 us (94%)
  local copies, waits for them, and re-layouts  1.38 us (5%)
    pallas_call x1, Pallas kernels, crossed(): pl.pallas_call(functools.partial(kernel, layers), out_shape=jax.ShapeDtyp...  23.8 us
    unnamed x1, local copies, waits for them, and re-layouts  1.38 us

profile of v5, /device:TPU:0, one launch (start us, length us, event | category | flops | bytes accessed | tf_op | source)
XLA Modules:
  0.0 25.1 jit_solution(6521755642872392241)
XLA Ops:
  0.0 23.8 %shard_map.55 = bf16[128,128]{1,0:T(8,128)(2,1)} custom-call(bf16[128,2048]{1,0:T(8,128)(2,1)} %bitcast.8, s32[8,128]{1,0:T(8,128)} %bitcast.12, s32[1,128]{1,0:T(1,128)} %bitcast.13, bf16[256,512]{1,0:T(8,128)(2,1)} %bitcast.9, bf16[256,512]{1,0:T(8,128)(2,1)} %bitcast.10), custom_call_target="tpu_custom_call" | custom-call | tf_op jit(solution)/shard_map/pallas_call | solution.py:282
  23.8 1.4 %copy.7 = bf16[1,1,128,128]{3,2,1,0:T(8,128)(2,1)} copy(bf16[1,1,128,128]{3,2,1,0:T(8,128)(2,1)} %bitcast.11) | data formatting | bytes 65536
